TPU v7x, 512 devices: a whole 4x8x8 slice. The times are simulated.
512 devices in a mesh: rows: 8 (over z), cols: 8 (over y), depth: 8 (over x, core).
Axes of the slice: x: 4, y: 8, z: 8, core: 2. Of those that a mesh axis runs over, the one named last changes fastest.
Arguments:
- tokens: bfloat16 [512, 12288], P(('rows', 'cols'), 'depth'), may hold values from -6 to 6
- weight_in: bfloat16 [12288, 49152], P('depth', ('rows', 'cols')), may hold values from -0.0546875 to 0.0546875
- bias_in: float32 [49152], P(('rows', 'cols')), may hold values from -4 to 4
- weight_out: bfloat16 [49152, 12288], P(('rows', 'cols'), 'depth'), may hold values from -0.02734375 to 0.02734375
- bias_out: float32 [12288], P('depth'), may hold values from -3 to 3
Outputs:
- output: bfloat16 [512, 12288], P(('rows', 'cols'), 'depth')
All inputs are finite; a program needn't handle non-finite values.
Results may differ from a plain program's by a relative error of at most 0.0046.
Values may be sent and summed in bfloat16 or wider, within the bound.
No kernel may reach another device: no remote copies, remote signals or barrier semaphores. Data moves between devices by JAX's collectives and lax.ppermute only.
A program may use at most 64 MiB of HBM per device.

v0:
```python
import jax
import jax.numpy as jnp
from jax import lax
from jax.sharding import PartitionSpec as P

PLANE = ("rows", "cols")


def shards(tokens, weight_in, bias_in, weight_out, bias_out):
    own = tokens.shape[0]
    planes = lax.axis_size(PLANE)
    gathered = lax.all_to_all(
        jnp.broadcast_to(tokens[None], (planes,) + tokens.shape), PLANE, 0, 0
    ).reshape(planes * own, -1)
    partial_hidden = jnp.dot(gathered, weight_in, preferred_element_type=jnp.float32)
    depths = lax.axis_size("depth")
    pieces = lax.all_to_all(
        partial_hidden.astype(jnp.bfloat16).reshape(depths, -1, weight_in.shape[1]), "depth", 0, 0
    )
    hidden = jnp.sum(pieces.astype(jnp.float32), axis=0) + bias_in
    active = jax.nn.gelu(hidden, approximate=True).astype(jnp.bfloat16)
    active = lax.all_gather(active, "depth", axis=0, tiled=True)
    partial_out = jnp.dot(active, weight_out, preferred_element_type=jnp.float32)
    parts = lax.all_to_all(partial_out.astype(jnp.bfloat16).reshape(planes, own, -1), PLANE, 0, 0)
    summed = jnp.sum(parts.astype(jnp.float32), axis=0)
    return (summed + bias_out).astype(jnp.bfloat16)


def solution(mesh):
    in_specs = (
        P(("rows", "cols"), "depth"),
        P("depth", ("rows", "cols")),
        P(("rows", "cols")),
        P(("rows", "cols"), "depth"),
        P("depth"),
    )
    out_specs = P(("rows", "cols"), "depth")
    return jax.shard_map(shards, mesh=mesh, in_specs=in_specs, out_specs=out_specs, check_vma=False)
```

profile of v0, /device:TPU:8, one launch (start us, length us, event | category | flops | bytes accessed | tf_op | source)
XLA Modules:
  0.0 142.8 jit_solution(7724320758658860799)
XLA Ops:
  0.0 0.0 copy-start
  0.0 1.0 broadcast_in_dim.2
  1.0 0.0 copy-start.3
  1.0 57.3 %all_to_all.15 = bf16[64,8,1536]{2,1,0:T(8,128)(2,1)S(1)} all-to-all(bf16[64,8,1536]{2,1,0:T(8,128)(2,1)S(1)} %broadcast_in_dim.2), channel_id=1, replica_groups=mesh['rows'=8,'cols'=8,'depth'=8] {'rows','cols'}, dimensions={0} | all-to-all | bytes 3145728 | tf_op jit(solution)/shard_map/all_to_all | solution.py:12
  58.3 0.0 copy-done.3
  58.3 1.4 fusion.3
  59.7 0.0 copy-start.2
  59.7 17.3 %all_to_all.16 = bf16[8,64,768]{2,1,0:T(8,128)(2,1)S(1)} all-to-all(bf16[8,64,768]{2,1,0:T(8,128)(2,1)S(1)} %bitcast.11), channel_id=1, replica_groups=mesh['rows'=8,'cols'=8,'depth'=8] {'depth'}, dimensions={0} | all-to-all | bytes 1572864 | tf_op jit(solution)/shard_map/all_to_all | solution.py:17
  77.0 0.1 convert_reduce_fusion.1
  77.1 0.0 copy-done.2
  77.1 0.1 fusion.13
  77.2 13.5 %all_gather.3 = bf16[512,768]{1,0:T(8,128)(2,1)S(1)} all-gather(bf16[64,768]{1,0:T(8,128)(2,1)S(1)} %fusion.13), channel_id=1, replica_groups=mesh['rows'=8,'cols'=8,'depth'=8] {'depth'}, dimensions={0}, use_global_device_ids=true | all-gather | bytes 884736 | tf_op jit(solution)/shard_map/all_gather | solution.py:22
  90.7 0.0 copy-done
  90.7 1.4 fusion
  92.1 49.4 %all_to_all.17 = bf16[64,8,1536]{2,1,0:T(8,128)(2,1)S(1)} all-to-all(bf16[64,8,1536]{2,1,0:T(8,128)(2,1)S(1)} %fusion), channel_id=1, replica_groups=mesh['rows'=8,'cols'=8,'depth'=8] {'rows','cols'}, dimensions={0} | all-to-all | bytes 3145728 | tf_op jit(solution)/shard_map/all_to_all | solution.py:24
  141.5 0.0 copy-start.1
  141.5 0.2 convert_reduce_fusion
  141.8 0.4 copy-done.1
  142.2 0.6 add_convert_fusion
Async XLA Ops:
  0.0 90.7 %copy-start = (bf16[768,1536]{1,0:T(8,128)(2,1)S(1)}, bf16[768,1536]{1,0:T(8,128)(2,1)}, u32[]{:S(2)}) copy-start(bf16[768,1536]{1,0:T(8,128)(2,1)} %param.8) | copy-start | bytes 7077892
  1.0 57.3 %copy-start.3 = (bf16[1536,768]{1,0:T(8,128)(2,1)S(1)}, bf16[1536,768]{1,0:T(8,128)(2,1)}, u32[]{:S(2)}) copy-start(bf16[1536,768]{1,0:T(8,128)(2,1)} %param.6) | copy-start | bytes 7077892
  59.7 17.5 %copy-start.2 = (f32[768]{0:T(1024)S(1)}, f32[768]{0:T(1024)}, u32[]{:S(2)}) copy-start(f32[768]{0:T(1024)} %param.7) | copy-start | bytes 9220
  141.5 0.7 copy-start.1
where the time goes:
time: 143 us
  blocking collectives  138 us (97%)
  matrix products  2.76 us (2%)
  local copies, waits for them, and re-layouts  1.45 us (1%)
    all_to_all x1, blocking collectives, shards(): lax.all_to_all(jnp.broadcast_to(tokens[None], (planes,) + tokens.shape),...  57.3 us
    all_to_all x1, blocking collectives, shards(): lax.all_to_all(partial_out.astype(jnp.bfloat16).reshape(planes, own, -1),...  49.4 us
    all_to_all x1, blocking collectives, shards(): lax.all_to_all(partial_hidden.astype(jnp.bfloat16).reshape(depths, -1, we...  17.3 us
    all_gather x1, blocking collectives, shards(): active = lax.all_gather(active, 'depth', axis=0, tiled=True)  13.5 us

commit v1 on v0

--- a/solution.py
+++ b/solution.py
@@ -19,7 +19,9 @@
     )
     hidden = jnp.sum(pieces.astype(jnp.float32), axis=0) + bias_in
     active = jax.nn.gelu(hidden, approximate=True).astype(jnp.bfloat16)
-    active = lax.all_gather(active, "depth", axis=0, tiled=True)
+    active = jnp.concatenate(
+        lax.all_to_all(jnp.stack([active] * lax.axis_size("depth")), "depth", 0, 0), axis=0
+    )
     partial_out = jnp.dot(active, weight_out, preferred_element_type=jnp.float32)
     parts = lax.all_to_all(partial_out.astype(jnp.bfloat16).reshape(planes, own, -1), PLANE, 0, 0)
     summed = jnp.sum(parts.astype(jnp.float32), axis=0)

time: 143 us -> 144 us (level)
    all_to_all x0 -> x1, blocking collectives: none -> 15.7 us  [shards(): lax.all_to_all(jnp.stack([active] * lax.axis_size('depth')), 'depth', 0, 0)]
    all_gather x1 -> x0, blocking collectives: 13.5 us -> none  [shards(): active = lax.all_gather(active, 'depth', axis=0, tiled=True)]
where the time goes in v1:
time: 144 us
  blocking collectives  139 us (97%)
  matrix products  2.76 us (2%)
  local copies, waits for them, and re-layouts  1.5 us (1%)
    all_to_all x1, blocking collectives, shards(): lax.all_to_all(jnp.broadcast_to(tokens[None], (planes,) + tokens.shape),...  57.3 us
    all_to_all x1, blocking collectives, shards(): lax.all_to_all(partial_out.astype(jnp.bfloat16).reshape(planes, own, -1),...  48.5 us
    all_to_all x1, blocking collectives, shards(): lax.all_to_all(partial_hidden.astype(jnp.bfloat16).reshape(depths, -1, we...  17.3 us
    all_to_all x1, blocking collectives, shards(): lax.all_to_all(jnp.stack([active] * lax.axis_size('depth')), 'depth', 0, 0)  15.7 us

profile of v1, /device:TPU:8, one launch (start us, length us, event | category | flops | bytes accessed | tf_op | source)
XLA Modules:
  0.0 144.1 jit_solution(8502085206370971451)
XLA Ops:
  0.0 0.0 copy-start
  0.0 1.0 broadcast_in_dim.2
  1.0 0.0 copy-start.3
  1.0 57.3 %all_to_all.20 = bf16[64,8,1536]{2,1,0:T(8,128)(2,1)S(1)} all-to-all(bf16[64,8,1536]{2,1,0:T(8,128)(2,1)S(1)} %broadcast_in_dim.2), channel_id=1, replica_groups=mesh['rows'=8,'cols'=8,'depth'=8] {'rows','cols'}, dimensions={0} | all-to-all | bytes 3145728 | tf_op jit(solution)/shard_map/all_to_all | solution.py:12
  58.3 0.0 copy-done.3
  58.3 1.4 fusion.3
  59.7 0.0 copy-start.2
  59.7 17.3 %all_to_all.21 = bf16[8,64,768]{2,1,0:T(8,128)(2,1)S(1)} all-to-all(bf16[8,64,768]{2,1,0:T(8,128)(2,1)S(1)} %bitcast.12), channel_id=1, replica_groups=mesh['rows'=8,'cols'=8,'depth'=8] {'depth'}, dimensions={0} | all-to-all | bytes 1572864 | tf_op jit(solution)/shard_map/all_to_all | solution.py:17
  77.0 0.1 convert_reduce_fusion.1
  77.1 0.0 copy-done.2
  77.1 0.1 fusion.13
  77.2 0.1 stack.2
  77.3 15.7 %all_to_all.22 = bf16[8,64,768]{2,1,0:T(8,128)(2,1)S(1)} all-to-all(bf16[8,64,768]{2,1,0:T(8,128)(2,1)S(1)} %stack.2), channel_id=1, replica_groups=mesh['rows'=8,'cols'=8,'depth'=8] {'depth'}, dimensions={0} | all-to-all | bytes 1572864 | tf_op jit(solution)/shard_map/all_to_all | solution.py:23
  92.9 0.0 copy-done
  92.9 1.4 fusion
  94.3 48.5 %all_to_all.23 = bf16[64,8,1536]{2,1,0:T(8,128)(2,1)S(1)} all-to-all(bf16[64,8,1536]{2,1,0:T(8,128)(2,1)S(1)} %fusion), channel_id=1, replica_groups=mesh['rows'=8,'cols'=8,'depth'=8] {'rows','cols'}, dimensions={0} | all-to-all | bytes 3145728 | tf_op jit(solution)/shard_map/all_to_all | solution.py:26
  142.8 0.0 copy-start.1
  142.8 0.2 convert_reduce_fusion
  143.1 0.4 copy-done.1
  143.5 0.6 add_convert_fusion
Async XLA Ops:
  0.0 92.9 %copy-start = (bf16[768,1536]{1,0:T(8,128)(2,1)S(1)}, bf16[768,1536]{1,0:T(8,128)(2,1)}, u32[]{:S(2)}) copy-start(bf16[768,1536]{1,0:T(8,128)(2,1)} %param.8) | copy-start | bytes 7077892
  1.0 57.3 %copy-start.3 = (bf16[1536,768]{1,0:T(8,128)(2,1)S(1)}, bf16[1536,768]{1,0:T(8,128)(2,1)}, u32[]{:S(2)}) copy-start(bf16[1536,768]{1,0:T(8,128)(2,1)} %param.6) | copy-start | bytes 7077892
  59.7 17.5 %copy-start.2 = (f32[768]{0:T(1024)S(1)}, f32[768]{0:T(1024)}, u32[]{:S(2)}) copy-start(f32[768]{0:T(1024)} %param.7) | copy-start | bytes 9220
  142.8 0.7 copy-start.1
